TPU v7x, 32 devices: a whole 2x2x4 slice. The times are simulated.
32 devices in a mesh: groups: 2 (over y), fsdp: 8 (over z, x), dp: 1, sub: 2 (over core).
Axes of the slice: x: 2, y: 2, z: 4, core: 2. Of those that a mesh axis runs over, the one named last changes fastest.
Arguments:
- features: bfloat16 [16, 768, 1280], P(('groups', 'fsdp', 'dp'), 'sub'), parts along dimension 0, may hold values from -6 to 6
- golden: bfloat16 [4, 768, 1280], P(('groups', 'dp'), 'sub'), parts along dimension 0, may hold values from -6 to 6
- die_wafer: int32 [16], P(('groups', 'fsdp', 'dp')), parts along dimension 0, may hold values from 0 to 1
- norm_gain: float32 [1280], replicated, may hold values from 0.1 to 1.9
- proj_weight: bfloat16 [1280, 2560], P('fsdp'), may hold values from -0.15625 to 0.15625
- out_weight: bfloat16 [2560, 1280], P('fsdp'), may hold values from -0.125 to 0.125
- zero_weight: bfloat16 [1280, 1280], P(None, 'fsdp'), may hold values from -0.15625 to 0.15625
Outputs:
- block_out: bfloat16 [16, 768, 1280], P(('groups', 'fsdp', 'dp'), 'sub'), parts along dimension 0
There are 2 independent parts, one for each index of `groups`. A program takes and returns all parts, laid end to end along the dimension named above; an argument that names none is the same for every part. Nothing has to cross between parts.
All inputs are finite; a program needn't handle non-finite values.
Results may differ from a plain program's by a relative error of at most 0.005.
Values may be sent and summed in bfloat16 or wider, within the bound.
A program may use at most 128 MiB of HBM per device.

v0:
```python
import jax
import jax.numpy as jnp
from jax import lax
from jax.sharding import PartitionSpec as P


def body(features, golden, die_wafer, norm_gain, proj_weight, out_weight, zero_weight):
    wafer_one = die_wafer[0]
    columns = jnp.einsum(
        "wpc,cd->wpd", golden, zero_weight, preferred_element_type=jnp.float32
    ).astype(jnp.bfloat16)
    gathered = lax.all_gather(columns, "fsdp", axis=2, tiled=True)
    residual = lax.dynamic_index_in_dim(gathered, wafer_one, 0, keepdims=False)
    mixed = features[0].astype(jnp.float32) + residual.astype(jnp.float32)
    average = jnp.mean(mixed, axis=-1, keepdims=True)
    centred = mixed - average
    variance = jnp.mean(centred * centred, axis=-1, keepdims=True)
    normed = (centred * lax.rsqrt(variance + 1e-05) * norm_gain).astype(jnp.bfloat16)
    inputs = normed
    preact = jnp.dot(
        inputs,
        lax.all_gather(proj_weight, "fsdp", axis=0, tiled=True),
        preferred_element_type=jnp.float32,
    )
    hidden = jax.nn.gelu(preact, approximate=True).astype(jnp.bfloat16)
    inputs = hidden
    branch = jnp.dot(
        inputs,
        lax.all_gather(out_weight, "fsdp", axis=0, tiled=True),
        preferred_element_type=jnp.float32,
    )
    return (mixed + branch).astype(jnp.bfloat16)[None]


def solution(mesh):
    placed = (
        P(("groups", "fsdp", "dp"), "sub", None),
        P(("groups", "dp"), "sub", None),
        P(("groups", "fsdp", "dp")),
        P(),
        P("fsdp", None),
        P("fsdp", None),
        P(None, "fsdp"),
    )
    return jax.shard_map(
        body,
        mesh=mesh,
        in_specs=placed,
        out_specs=P(("groups", "fsdp", "dp"), "sub", None),
        check_vma=False,
    )
```

profile of v0, /device:TPU:0, one launch (start us, length us, event | category | flops | bytes accessed | tf_op | source)
XLA Modules:
  0.0 289.0 jit_solution(17761163579044327469)
XLA Ops:
  6.5 0.0 copy-start
  6.5 0.0 all-gather.4.cloned.1.call-start
  6.5 1.5 copy-done
  8.1 2.5 convolution_convert_fusion
  10.6 0.0 all-gather.4.cloned.1.call-update
  10.6 0.0 all-gather.6.cloned.1.call-start
  10.7 0.7 all-gather.6.cloned.1.call-update
  11.4 0.0 all-gather.8.cloned.1.call-start
  11.4 0.7 all-gather.8.cloned.1.call-update
  12.7 1.6 copy.8
  14.3 46.6 %all-gather.4.cloned.1.call-done = bf16[2,384,1280]{1,2,0:T(8,128)(2,1)} async-done(((bf16[2,384,160]{1,2,0:T(8,128)(2,1)}), bf16[2,384,1280]{1,2,0:T(8,128)(2,1)}) %all-gather.4.cloned.1.call-update) | async-done | bytes 1966096 | tf_op jit(solution)/shard_map/all_gather | solution.py:12
  61.0 0.0 copy-start.1
  61.0 0.0 copy-start.2
  61.0 1.7 fusion.15
  62.7 0.1 copy-done.1
  62.8 0.4 multiply_reduce_fusion
  63.3 101.3 %all-gather.6.cloned.1.call-done = bf16[1280,2560]{1,0:T(8,128)(2,1)} async-done(((bf16[160,2560]{1,0:T(8,128)(2,1)}), bf16[1280,2560]{1,0:T(8,128)(2,1)}) %all-gather.6.cloned.1.call-update) | async-done | bytes 6553616 | tf_op jit(solution)/shard_map/all_gather | solution.py:22
  164.5 102.6 %all-gather.8.cloned.1.call-done = bf16[2560,1280]{1,0:T(8,128)(2,1)} async-done(((bf16[320,1280]{1,0:T(8,128)(2,1)}), bf16[2560,1280]{1,0:T(8,128)(2,1)}) %all-gather.8.cloned.1.call-update) | async-done | bytes 6553616 | tf_op jit(solution)/shard_map/all_gather | solution.py:29
  267.2 0.0 copy-done.2
  267.2 13.0 %fusion.9 = bf16[1,384,1280]{1,2,0:T(8,128)(2,1)} fusion(bf16[2560,1280]{1,0:T(8,128)(2,1)} %all-gather.8.cloned.1.call-done, bf16[1,384,1280]{1,2,0:T(8,128)(2,1)S(1)} %copy.8, bf16[1280,2560]{1,0:T(8,128)(2,1)} %all-gather.6.cloned.1.call-done, f32[1280]{0:T(1024)S(1)} %copy-done.2, f32[384]{0:T(512)S(1)} %add_rsqrt_fusion, ...), kind=kOutput, calls=%fused_computation.11 | convolution fusion | flops 5047910400 | bytes 18035712 | tf_op jit(solution)/shard_map/dot_general | solution.py:27
  280.2 2.2 copy.10
  (2 shorter events, 0.0 us)
Async XLA Ops:
  6.5 1.5 copy-start
  6.5 54.4 %all-gather.4.cloned.1.call-start = ((), (), s32[]{:S(2)}) async-start(), calls=%async_computation | async-start | bytes 2211840 | tf_op jit(solution)/shard_map/all_gather | solution.py:12
  10.6 153.9 %all-gather.6.cloned.1.call-start = ((), (), s32[]{:S(2)}) async-start(), calls=%async_computation.1 | async-start | bytes 7372800 | tf_op jit(solution)/shard_map/all_gather | solution.py:22
  11.4 255.8 %all-gather.8.cloned.1.call-start = ((), (), s32[]{:S(2)}) async-start(), calls=%async_computation.2 | async-start | bytes 7372800 | tf_op jit(solution)/shard_map/all_gather | solution.py:29
  61.0 1.8 copy-start.1
  61.0 206.2 %copy-start.2 = (f32[1280]{0:T(1024)S(1)}, f32[1280]{0:T(1024)}, u32[]{:S(2)}) copy-start(f32[1280]{0:T(1024)} %param.10) | copy-start | bytes 15364
Sparse Core Ops, SparseCore 0:
  10.7 50.2 all-gather.3
  63.2 101.3 all-gather.5
  166.7 100.3 all-gather.7
where the time goes:
time: 289 us
  waiting for transfers between devices  252 us (87%)
  matrix products  15.5 us (5%)
  between operations  13.8 us (5%)
  local copies, waits for them, and re-layouts  5.51 us (2%)
    all_gather x1, waiting for transfers between devices, body(): lax.all_gather(out_weight, 'fsdp', axis=0, tiled=True)  103 us
    all_gather x1, waiting for transfers between devices, body(): lax.all_gather(proj_weight, 'fsdp', axis=0, tiled=True)  101 us
    all_gather x1, waiting for transfers between devices, body(): gathered = lax.all_gather(columns, 'fsdp', axis=2, tiled=True)  46.6 us
    dot_general x1, matrix products, body(): jnp.dot(inputs, lax.all_gather(out_weight, 'fsdp', axis=0, tiled=True), p...  13 us
  transfers between devices with their start and end apart: 3, of which 3 were waited for; matrix products, arithmetic and copies ran while one was open for 1% of the time, Pallas kernels for 0%

commit v1 on v0

v1 whole, which is shorter than its diff:
```python
import functools

import jax
import jax.numpy as jnp
from jax import lax
from jax.experimental import pallas as pl
from jax.experimental.pallas import tpu as pltpu
from jax.sharding import PartitionSpec as P

MESH = pl.DeviceIdType.MESH
TILE = 256


def kernel(n, snake, die_ref, gain_ref, feat_hbm, gold_hbm, z_hbm, p_hbm, o_hbm, out_ref,
           feat, gold, zb, pb, ob, mixed, normed, hidden,
           ring_send, ring_recv, y_send, y_recv, sib_send, sib_recv, local_sem):
    y = lax.axis_index("groups")
    me = lax.axis_index("fsdp")
    core = lax.axis_index("sub")
    steps = n - 1
    rows, width = feat.shape
    ff = hidden.shape[1]
    rp = z_hbm.shape[0]
    ro = o_hbm.shape[0]

    def place_of(idx):
        if not snake:
            return idx
        half, odd = lax.div(idx, 2), lax.rem(idx, 2)
        return half * (1 - odd) + odd * (n - 1 - half)

    def index_at(place):
        if not snake:
            return place
        back = lax.div(place, n // 2)
        return (1 - back) * 2 * place + back * (2 * (n - 1 - place) + 1)

    here = place_of(me)

    def at(shift):
        return index_at(lax.rem(here + shift + 2 * n, n))

    ahead, behind = {"fsdp": at(1)}, {"fsdp": at(-1)}
    across, sibling = {"groups": 1 - y}, {"sub": 1 - core}

    locals_ = [
        pltpu.make_async_copy(p_hbm, pb.at[pl.ds(pl.multiple_of(me * rp, 16), rp), :], local_sem.at[0]),
        pltpu.make_async_copy(z_hbm, zb.at[pl.ds(pl.multiple_of(me * rp, 16), rp), :], local_sem.at[1]),
        pltpu.make_async_copy(o_hbm, ob.at[pl.ds(pl.multiple_of(me * ro, 16), ro), :], local_sem.at[2]),
        pltpu.make_async_copy(gold_hbm, gold, local_sem.at[3]),
        pltpu.make_async_copy(feat_hbm, feat, local_sem.at[4]),
    ]
    for copy in locals_:
        copy.start()

    barrier = pltpu.get_barrier_semaphore()
    for other in (ahead, behind, across, sibling):
        pl.semaphore_signal(barrier, inc=1, device_id=other, device_id_type=MESH)
    for copy in locals_[:3]:
        copy.wait()
    pl.semaphore_wait(barrier, 4)

    first = (width // TILE + 1) // 2 * TILE
    half = width // 2
    ru = rp // 16
    qu = ro // 2 // 16
    streams = [
        (zb, rp, 0, rp, 0, half, half, ru // 3 * 16),
        (pb, rp, 0, rp, 0, ff // 4, ff // 4, ru // 3 * 16),
        (pb, rp, 0, rp, ff // 2, ff // 4, ff // 4, ru // 3 * 16),
        (ob, ro, ro // 2, ro // 2, 0, 0, first, (qu + 2) // 3 * 16),
        (ob, ro, ro // 2, ro // 2, first, 0, width - first, (qu + 2) // 3 * 16),
    ]

    def piece(j, owner, part, who):
        buf, per, core_rows, count, col, core_cols, cols, outer = streams[j]
        row = owner * per + who * core_rows
        if part == 0:
            row, size = row + y * (count - outer), outer
        elif part == 1:
            row, size = row + outer, count - 2 * outer
        else:
            row, size = row + (1 - y) * (count - outer), outer
        start = col + who * core_cols if core_cols else col
        if core_cols:
            start = pl.multiple_of(start, 128)
        return buf.at[pl.ds(pl.multiple_of(row, 16), size), pl.ds(start, cols)]

    pending = []

    def remote(ref, send, recv, to):
        return pltpu.make_async_remote_copy(
            src_ref=ref, dst_ref=ref, send_sem=send, recv_sem=recv, device_id=to, device_id_type=MESH)

    def send(ref, s, r, to):
        copy = remote(ref, s, r, to)
        copy.start()
        pending.append(copy)

    def came(ref, s, r, to):
        remote(ref, s, r, to).wait_recv()

    def to_sibling(j, t, part, owner):
        send(piece(j, owner, part, core), sib_send.at[j, t, part], sib_recv.at[j, t, part], sibling)

    def event(j, s):
        if s == 0:
            send(piece(j, me, 0, core), ring_send.at[j, 0, 0], ring_recv.at[j, 0, 0], ahead)
            send(piece(j, me, 1, core), ring_send.at[j, 0, 1], ring_recv.at[j, 0, 1], behind)
            return
        t = s - 1
        if t < steps:
            owner = at(-1 - t)
            ref = piece(j, owner, 0, core)
            came(ref, ring_send.at[j, t, 0], ring_recv.at[j, t, 0], ahead)
            if s < steps:
                send(ref, ring_send.at[j, s, 0], ring_recv.at[j, s, 0], ahead)
            send(ref, y_send.at[j, t], y_recv.at[j, t], across)
            to_sibling(j, t, 0, owner)
            owner = at(1 + t)
            ref = piece(j, owner, 1, core)
            came(ref, ring_send.at[j, t, 1], ring_recv.at[j, t, 1], behind)
            if s < steps:
                send(ref, ring_send.at[j, s, 1], ring_recv.at[j, s, 1], behind)
            to_sibling(j, t, 1, owner)
        if t >= 1:
            owner = at(-t)
            came(piece(j, owner, 2, core), y_send.at[j, t - 1], y_recv.at[j, t - 1], across)
            to_sibling(j, t - 1, 2, owner)

    def arrived(j):
        for t in range(steps):
            for part, owner in ((0, at(-1 - t)), (1, at(1 + t)), (2, at(-1 - t))):
                came(piece(j, owner, part, 1 - core), sib_send.at[j, t, part], sib_recv.at[j, t, part], sibling)

    wafer = die_ref[0]

    def control():
        arrived(0)
        locals_[3].wait()
        locals_[4].wait()

        @pl.loop(0, width // TILE)
        def _(i):
            cols = pl.ds(pl.multiple_of(i * TILE, TILE), TILE)
            residual = lax.dot_general(
                gold[wafer], zb[cols, :], (((1,), (1,)), ((), ())), preferred_element_type=jnp.float32
            ).astype(jnp.bfloat16)
            mixed[:, cols] = feat[:, cols].astype(jnp.float32) + residual.astype(jnp.float32)

    def norm():
        gain = gain_ref[...]

        @pl.loop(0, rows // 32)
        def _(i):
            part = pl.ds(pl.multiple_of(i * 32, 32), 32)
            value = mixed[part, :]
            centred = value - jnp.mean(value, axis=-1, keepdims=True)
            variance = jnp.mean(centred * centred, axis=-1, keepdims=True)
            normed[part, :] = (centred * lax.rsqrt(variance + 1e-05) * gain).astype(jnp.bfloat16)

    def project(low, high):
        @pl.loop(low // TILE, high // TILE)
        def _(i):
            cols = pl.ds(pl.multiple_of(i * TILE, TILE), TILE)
            preact = jnp.dot(normed[...], pb[:, cols], preferred_element_type=jnp.float32)
            hidden[:, cols] = jax.nn.gelu(preact, approximate=True).astype(jnp.bfloat16)

    def output(low, high):
        @pl.loop(low // TILE, high // TILE)
        def _(i):
            cols = pl.ds(pl.multiple_of(i * TILE, TILE), TILE)
            branch = jnp.dot(hidden[...], ob[:, cols], preferred_element_type=jnp.float32)
            out_ref[:, cols] = (mixed[:, cols] + branch).astype(jnp.bfloat16)

    scale = steps / 7
    starts = (0.0, 0.5, 14.0 * scale, 14.3 * scale, 14.6 * scale)
    paces = (2.0, 2.0, 2.2, 2.7, 3.0)
    plan = [(starts[j] + paces[j] * s, j, functools.partial(event, j, s)) for j in range(5) for s in range(n + 1)]

    def end(j):
        return starts[j] + paces[j] * n

    plan += [
        (end(0) + 2.1, 9, control),
        (end(0) + 3.1, 9, norm),
        (end(1) + 4.1, 9, lambda: (arrived(1), project(0, ff // 4 // TILE * TILE))),
        (end(1) + 6.1, 9, lambda: project(ff // 4 // TILE * TILE, ff // 2)),
        (end(2) + 2.1, 9, lambda: (arrived(2), project(ff // 2, ff // 2 + ff // 4 // TILE * TILE))),
        (end(2) + 3.1, 9, lambda: project(ff // 2 + ff // 4 // TILE * TILE, ff)),
        (end(3) + 2.1, 9, lambda: (arrived(3), output(0, first))),
        (end(4) + 9.1, 9, lambda: (arrived(4), output(first, width))),
    ]
    for _, _, act in sorted(plan, key=lambda item: item[:2]):
        act()
    for copy in pending:
        copy.wait_send()


def body(n, snake, features, golden, die_wafer, norm_gain, proj_weight, out_weight, zero_weight):
    rows, width = features.shape[1:]
    ff = proj_weight.shape[1]
    dma = pltpu.SemaphoreType.DMA
    anywhere = pl.BlockSpec(memory_space=pl.ANY)
    out = pl.pallas_call(
        functools.partial(kernel, n, snake),
        out_shape=jax.ShapeDtypeStruct((rows, width), jnp.bfloat16),
        in_specs=[pl.BlockSpec(memory_space=pltpu.SMEM), pl.BlockSpec(memory_space=pltpu.VMEM)] + [anywhere] * 5,
        out_specs=pl.BlockSpec(memory_space=pltpu.VMEM),
        scratch_shapes=[
            pltpu.VMEM((rows, width), jnp.bfloat16),
            pltpu.VMEM(golden.shape, jnp.bfloat16),
            pltpu.VMEM((width, width), jnp.bfloat16),
            pltpu.VMEM((width, ff), jnp.bfloat16),
            pltpu.VMEM((ff, width), jnp.bfloat16),
            pltpu.VMEM((rows, width), jnp.float32),
            pltpu.VMEM((rows, width), jnp.bfloat16),
            pltpu.VMEM((rows, ff), jnp.bfloat16),
            dma((5, n - 1, 2)), dma((5, n - 1, 2)),
            dma((5, n - 1)), dma((5, n - 1)),
            dma((5, n - 1, 3)), dma((5, n - 1, 3)),
            dma((5,)),
        ],
        compiler_params=pltpu.CompilerParams(
            collective_id=0, has_side_effects=True, vmem_limit_bytes=48 * 1024 * 1024),
    )(die_wafer, norm_gain[None], features[0], golden, zero_weight.T, proj_weight, out_weight)
    return out[None]


def solution(mesh):
    placed = (
        P(("groups", "fsdp", "dp"), "sub", None),
        P(("groups", "dp"), "sub", None),
        P(("groups", "fsdp", "dp")),
        P(),
        P("fsdp", None),
        P("fsdp", None),
        P(None, "fsdp"),
    )
    return jax.shard_map(
        functools.partial(body, mesh.shape["fsdp"], mesh.shape["dp"] == 1),
        mesh=mesh,
        in_specs=placed,
        out_specs=P(("groups", "fsdp", "dp"), "sub", None),
        check_vma=False,
    )
```

time: 289 us -> 90.7 us (0.31)
  waiting for transfers between devices: 252 us -> 0 us
  Pallas kernels: 0 us -> 82 us
  matrix products: 15.5 us -> 0 us
  between operations: 13.8 us -> 0.67 us
    all_gather x3 -> x0, waiting for transfers between devices: 251 us -> none  [the longest x1 103 us: body(): lax.all_gather(out_weight, 'fsdp', axis=0, tiled=True)]
    pallas_call x0 -> x1, Pallas kernels: none -> 82 us  [body(): pl.pallas_call(functools.partial(kernel, n, snake), out_shape=jax.ShapeDt...]
    dot_general x2 -> x0, matrix products: 15.5 us -> none  [the longest x1 13 us: body(): jnp.dot(inputs, lax.all_gather(out_weight, 'fsdp', axis=0, tiled=True), p...]
    unnamed x7 -> x11, local copies, waits for them, and re-layouts: 3.28 us -> 6.98 us
  transfers between devices with their start and end apart: 3 -> 0, of which waited for: 3 -> 0; matrix products, arithmetic and copies ran while one was open for 1% -> 0% of each run, Pallas kernels for 0% -> 0%
where the time goes in v1:
time: 90.7 us; the launch traced here: 90.3 us
  Pallas kernels  82 us (90%)
  local copies, waits for them, and re-layouts  7.68 us (8%)
    pallas_call x1, Pallas kernels, body(): pl.pallas_call(functools.partial(kernel, n, snake), out_shape=jax.ShapeDt...  82 us
    unnamed x11, local copies, waits for them, and re-layouts  6.98 us

profile of v1, /device:TPU:0, one launch (start us, length us, event | category | flops | bytes accessed | tf_op | source)
XLA Modules:
  0.0 90.3 jit_solution(8826166270705293576)
XLA Ops:
  0.7 0.7 broadcast_in_dim.6.gain_ref
  1.4 0.0 copy-start
  1.4 1.5 %copy-done = bf16[2,384,1280]{2,1,0:T(8,128)(2,1)S(1)} copy-done((bf16[2,384,1280]{2,1,0:T(8,128)(2,1)S(1)}, bf16[2,384,1280]{2,1,0:T(8,128)(2,1)}, u32[]{:S(2)}) %copy-start) | copy-done | bytes 1966104
  2.9 0.0 copy-start.1
  2.9 1.2 %copy-done.1 = bf16[1,384,1280]{2,1,0:T(8,128)(2,1)S(1)} copy-done((bf16[1,384,1280]{2,1,0:T(8,128)(2,1)S(1)}, bf16[1,384,1280]{2,1,0:T(8,128)(2,1)}, u32[]{:S(2)}) %copy-start.1) | copy-done | bytes 983064
  4.1 0.0 copy-start.2
  4.1 1.1 %copy-done.2 = bf16[160,2560]{1,0:T(8,128)(2,1)S(1)} copy-done((bf16[160,2560]{1,0:T(8,128)(2,1)S(1)}, bf16[160,2560]{1,0:T(8,128)(2,1)}, u32[]{:S(2)}) %copy-start.2) | copy-done | bytes 819224
  5.2 0.0 copy-start.3
  5.2 1.1 %copy-done.3 = bf16[320,1280]{1,0:T(8,128)(2,1)S(1)} copy-done((bf16[320,1280]{1,0:T(8,128)(2,1)S(1)}, bf16[320,1280]{1,0:T(8,128)(2,1)}, u32[]{:S(2)}) %copy-start.3) | copy-done | bytes 819224
  6.4 0.0 copy-start.4
  6.4 1.0 %copy-done.4 = bf16[1280,160]{0,1:T(8,128)(2,1)S(1)} copy-done((bf16[1280,160]{0,1:T(8,128)(2,1)S(1)}, bf16[1280,160]{0,1:T(8,128)(2,1)}, u32[]{:S(2)}) %copy-start.4) | copy-done | bytes 409624
  7.4 82.0 %shard_map.73 = bf16[384,1280]{1,0:T(8,128)(2,1)S(1)} custom-call(s32[1]{0:T(128)S(6)} %copy.9.die_ref, f32[1,1280]{1,0:T(1,128)S(1)} %broadcast_in_dim.6.gain_ref, bf16[384,1280]{1,0:T(8,128)(2,1)S(1)} %bitcast.4, bf16[2,384,1280]{2,1,0:T(8,128)(2,1)S(1)} %copy-done, bf16[160,1280]{1,0:T(8,128)(2,1)S(1)} %bitcast.5, bf16[160,2560]{1,0:T(8,128)(2,1)S(1)} %copy-done.2, ...), custom_call_target="tpu_custom_call" | custom-call | tf_op jit(solution)/shard_map/pallas_call | solution.py:205
  89.4 0.9 %copy.10 = bf16[1,384,1280]{2,1,0:T(8,128)(2,1)} copy(bf16[1,384,1280]{2,1,0:T(8,128)(2,1)S(1)} %bitcast.3) | data formatting | bytes 1966080
Async XLA Ops:
  1.4 1.5 %copy-start = (bf16[2,384,1280]{2,1,0:T(8,128)(2,1)S(1)}, bf16[2,384,1280]{2,1,0:T(8,128)(2,1)}, u32[]{:S(2)}) copy-start(bf16[2,384,1280]{2,1,0:T(8,128)(2,1)} %gold_hbm.1) | copy-start | bytes 5898244
  2.9 1.2 %copy-start.1 = (bf16[1,384,1280]{2,1,0:T(8,128)(2,1)S(1)}, bf16[1,384,1280]{2,1,0:T(8,128)(2,1)}, u32[]{:S(2)}) copy-start(bf16[1,384,1280]{2,1,0:T(8,128)(2,1)} %param.7) | copy-start | bytes 2949124
  4.1 1.1 %copy-start.2 = (bf16[160,2560]{1,0:T(8,128)(2,1)S(1)}, bf16[160,2560]{1,0:T(8,128)(2,1)}, u32[]{:S(2)}) copy-start(bf16[160,2560]{1,0:T(8,128)(2,1)} %p_hbm.1) | copy-start | bytes 2457604
  5.2 1.1 %copy-start.3 = (bf16[320,1280]{1,0:T(8,128)(2,1)S(1)}, bf16[320,1280]{1,0:T(8,128)(2,1)}, u32[]{:S(2)}) copy-start(bf16[320,1280]{1,0:T(8,128)(2,1)} %o_hbm.1) | copy-start | bytes 2457604
  6.4 1.0 %copy-start.4 = (bf16[1280,160]{0,1:T(8,128)(2,1)S(1)}, bf16[1280,160]{0,1:T(8,128)(2,1)}, u32[]{:S(2)}) copy-start(bf16[1280,160]{0,1:T(8,128)(2,1)} %param.13) | copy-start | bytes 1228804

commit v2 on v1

--- a/solution.py
+++ b/solution.py
@@ -9,6 +9,12 @@
 
 MESH = pl.DeviceIdType.MESH
 TILE = 256
+STREAMS = (("z", 0, 5), ("p", 0, 5), ("p", 5, 10), ("o", 0, 3), ("o", 3, 5))
+STARTS = (0, 0.2, 0.4, 6.0, 7.0)
+PACES = (3.0, 3.6, 4.2, 4.1, 4.1)
+DELAYS = (2.0, 2.0, 2.0, 2.0, 9.0)
+GROUP = 1
+GAP = 1.0
 
 
 def kernel(n, snake, die_ref, gain_ref, feat_hbm, gold_hbm, z_hbm, p_hbm, o_hbm, out_ref,
@@ -37,8 +43,13 @@
 
     here = place_of(me)
 
+    around = {}
+
     def at(shift):
-        return index_at(lax.rem(here + shift + 2 * n, n))
+        shift %= n
+        if shift not in around:
+            around[shift] = index_at(lax.rem(here + shift, n))
+        return around[shift]
 
     ahead, behind = {"fsdp": at(1)}, {"fsdp": at(-1)}
     across, sibling = {"groups": 1 - y}, {"sub": 1 - core}
@@ -60,17 +71,17 @@
         copy.wait()
     pl.semaphore_wait(barrier, 4)
 
-    first = (width // TILE + 1) // 2 * TILE
-    half = width // 2
     ru = rp // 16
     qu = ro // 2 // 16
-    streams = [
-        (zb, rp, 0, rp, 0, half, half, ru // 3 * 16),
-        (pb, rp, 0, rp, 0, ff // 4, ff // 4, ru // 3 * 16),
-        (pb, rp, 0, rp, ff // 2, ff // 4, ff // 4, ru // 3 * 16),
-        (ob, ro, ro // 2, ro // 2, 0, 0, first, (qu + 2) // 3 * 16),
-        (ob, ro, ro // 2, ro // 2, first, 0, width - first, (qu + 2) // 3 * 16),
-    ]
+
+    def stream(kind, low, high):
+        low, high = low * TILE, high * TILE
+        if kind == "o":
+            return ob, ro, ro // 2, ro // 2, low, 0, high - low, (qu + 2) // 3 * 16
+        half = (high - low) // 2
+        return {"z": zb, "p": pb}[kind], rp, 0, rp, low, half, half, ru // 3 * 16
+
+    streams = [stream(*item) for item in STREAMS]
 
     def piece(j, owner, part, who):
         buf, per, core_rows, count, col, core_cols, cols, outer = streams[j]
@@ -135,21 +146,21 @@
 
     wafer = die_ref[0]
 
-    def control():
-        arrived(0)
-        locals_[3].wait()
-        locals_[4].wait()
-
-        @pl.loop(0, width // TILE)
-        def _(i):
-            cols = pl.ds(pl.multiple_of(i * TILE, TILE), TILE)
-            residual = lax.dot_general(
-                gold[wafer], zb[cols, :], (((1,), (1,)), ((), ())), preferred_element_type=jnp.float32
-            ).astype(jnp.bfloat16)
-            mixed[:, cols] = feat[:, cols].astype(jnp.float32) + residual.astype(jnp.float32)
+    def tiles(low, high, step):
+        def loop():
+            @pl.loop(low, high)
+            def _(i):
+                step(pl.ds(pl.multiple_of(i * TILE, TILE), TILE))
+        return loop
+
+    def control(cols):
+        residual = lax.dot_general(
+            gold[wafer], zb[cols, :], (((1,), (1,)), ((), ())), preferred_element_type=jnp.float32
+        ).astype(jnp.bfloat16)
+        mixed[:, cols] = feat[:, cols].astype(jnp.float32) + residual.astype(jnp.float32)
 
     def norm():
-        gain = gain_ref[...]
+        gain = gain_ref[...][None]
 
         @pl.loop(0, rows // 32)
         def _(i):
@@ -159,38 +170,31 @@
             variance = jnp.mean(centred * centred, axis=-1, keepdims=True)
             normed[part, :] = (centred * lax.rsqrt(variance + 1e-05) * gain).astype(jnp.bfloat16)
 
-    def project(low, high):
-        @pl.loop(low // TILE, high // TILE)
-        def _(i):
-            cols = pl.ds(pl.multiple_of(i * TILE, TILE), TILE)
-            preact = jnp.dot(normed[...], pb[:, cols], preferred_element_type=jnp.float32)
-            hidden[:, cols] = jax.nn.gelu(preact, approximate=True).astype(jnp.bfloat16)
-
-    def output(low, high):
-        @pl.loop(low // TILE, high // TILE)
-        def _(i):
-            cols = pl.ds(pl.multiple_of(i * TILE, TILE), TILE)
-            branch = jnp.dot(hidden[...], ob[:, cols], preferred_element_type=jnp.float32)
-            out_ref[:, cols] = (mixed[:, cols] + branch).astype(jnp.bfloat16)
+    def project(cols):
+        preact = jnp.dot(normed[...], pb[:, cols], preferred_element_type=jnp.float32)
+        hidden[:, cols] = jax.nn.gelu(preact, approximate=True).astype(jnp.bfloat16)
+
+    def output(cols):
+        branch = jnp.dot(hidden[...], ob[:, cols], preferred_element_type=jnp.float32)
+        out_ref[:, cols] = (mixed[:, cols] + branch).astype(jnp.bfloat16)
 
     scale = steps / 7
-    starts = (0.0, 0.5, 14.0 * scale, 14.3 * scale, 14.6 * scale)
-    paces = (2.0, 2.0, 2.2, 2.7, 3.0)
-    plan = [(starts[j] + paces[j] * s, j, functools.partial(event, j, s)) for j in range(5) for s in range(n + 1)]
-
-    def end(j):
-        return starts[j] + paces[j] * n
-
-    plan += [
-        (end(0) + 2.1, 9, control),
-        (end(0) + 3.1, 9, norm),
-        (end(1) + 4.1, 9, lambda: (arrived(1), project(0, ff // 4 // TILE * TILE))),
-        (end(1) + 6.1, 9, lambda: project(ff // 4 // TILE * TILE, ff // 2)),
-        (end(2) + 2.1, 9, lambda: (arrived(2), project(ff // 2, ff // 2 + ff // 4 // TILE * TILE))),
-        (end(2) + 3.1, 9, lambda: project(ff // 2 + ff // 4 // TILE * TILE, ff)),
-        (end(3) + 2.1, 9, lambda: (arrived(3), output(0, first))),
-        (end(4) + 9.1, 9, lambda: (arrived(4), output(first, width))),
-    ]
+    count = len(STREAMS)
+    plan = [(STARTS[j] * scale + PACES[j] * s, j, functools.partial(event, j, s)) for j in range(count) for s in range(n + 1)]
+    clock = 0.0
+    for j, (kind, low, high) in enumerate(STREAMS):
+        clock = max(clock, STARTS[j] * scale + PACES[j] * n + DELAYS[j])
+        acts = [functools.partial(arrived, j)]
+        if j == 0:
+            acts += [locals_[3].wait, locals_[4].wait]
+        step = {"z": control, "p": project, "o": output}[kind]
+        acts += [tiles(i, min(i + GROUP, high), step) for i in range(low, high, GROUP)]
+        if kind == "z":
+            acts.append(norm)
+        for act in acts:
+            plan.append((clock, 99, act))
+            if act not in acts[:1]:
+                clock += GAP
     for _, _, act in sorted(plan, key=lambda item: item[:2]):
         act()
     for copy in pending:
@@ -201,7 +205,8 @@
     rows, width = features.shape[1:]
     ff = proj_weight.shape[1]
     dma = pltpu.SemaphoreType.DMA
-    anywhere = pl.BlockSpec(memory_space=pl.ANY)
+    count = len(STREAMS)
+    anywhere = pl.BlockSpec(memory_space=pltpu.HBM)
     out = pl.pallas_call(
         functools.partial(kernel, n, snake),
         out_shape=jax.ShapeDtypeStruct((rows, width), jnp.bfloat16),
@@ -216,14 +221,14 @@
             pltpu.VMEM((rows, width), jnp.float32),
             pltpu.VMEM((rows, width), jnp.bfloat16),
             pltpu.VMEM((rows, ff), jnp.bfloat16),
-            dma((5, n - 1, 2)), dma((5, n - 1, 2)),
-            dma((5, n - 1)), dma((5, n - 1)),
-            dma((5, n - 1, 3)), dma((5, n - 1, 3)),
+            dma((count, n - 1, 2)), dma((count, n - 1, 2)),
+            dma((count, n - 1)), dma((count, n - 1)),
+            dma((count, n - 1, 3)), dma((count, n - 1, 3)),
             dma((5,)),
         ],
         compiler_params=pltpu.CompilerParams(
             collective_id=0, has_side_effects=True, vmem_limit_bytes=48 * 1024 * 1024),
-    )(die_wafer, norm_gain[None], features[0], golden, zero_weight.T, proj_weight, out_weight)
+    )(die_wafer, norm_gain, features[0], golden, zero_weight.T, proj_weight, out_weight)
     return out[None]
 
 

time: 90.7 us -> 84.9 us (0.936)
  Pallas kernels: 82 us -> 76.2 us
    pallas_call x1, Pallas kernels: 82 us -> 76.2 us  [body(): pl.pallas_call(functools.partial(kernel, n, snake), out_shape=jax.ShapeDt...]
    unnamed x11 -> x13, local copies, waits for them, and re-layouts: 6.98 us -> 7.67 us
where the time goes in v2:
time: 84.9 us; the launch traced here: 84.5 us
  Pallas kernels  76.2 us (90%)
  local copies, waits for them, and re-layouts  7.67 us (9%)
    pallas_call x1, Pallas kernels, body(): pl.pallas_call(functools.partial(kernel, n, snake), out_shape=jax.ShapeDt...  76.2 us
    unnamed x13, local copies, waits for them, and re-layouts  7.67 us

profile of v2, /device:TPU:0, one launch (start us, length us, event | category | flops | bytes accessed | tf_op | source)
XLA Modules:
  0.0 84.5 jit_solution(15534194294084539077)
XLA Ops:
  0.7 0.0 copy-start
  0.7 1.5 %copy-done = bf16[2,384,1280]{2,1,0:T(8,128)(2,1)S(1)} copy-done((bf16[2,384,1280]{2,1,0:T(8,128)(2,1)S(1)}, bf16[2,384,1280]{2,1,0:T(8,128)(2,1)}, u32[]{:S(2)}) %copy-start) | copy-done | bytes 1966104
  2.2 0.0 copy-start.1
  2.2 1.2 %copy-done.1 = bf16[1,384,1280]{2,1,0:T(8,128)(2,1)S(1)} copy-done((bf16[1,384,1280]{2,1,0:T(8,128)(2,1)S(1)}, bf16[1,384,1280]{2,1,0:T(8,128)(2,1)}, u32[]{:S(2)}) %copy-start.1) | copy-done | bytes 983064
  3.4 0.0 copy-start.2
  3.4 1.1 %copy-done.2 = bf16[160,2560]{1,0:T(8,128)(2,1)S(1)} copy-done((bf16[160,2560]{1,0:T(8,128)(2,1)S(1)}, bf16[160,2560]{1,0:T(8,128)(2,1)}, u32[]{:S(2)}) %copy-start.2) | copy-done | bytes 819224
  4.5 0.0 copy-start.3
  4.5 1.1 %copy-done.3 = bf16[320,1280]{1,0:T(8,128)(2,1)S(1)} copy-done((bf16[320,1280]{1,0:T(8,128)(2,1)S(1)}, bf16[320,1280]{1,0:T(8,128)(2,1)}, u32[]{:S(2)}) %copy-start.3) | copy-done | bytes 819224
  5.7 0.0 copy-start.4
  5.7 1.0 %copy-done.4 = bf16[1280,160]{0,1:T(8,128)(2,1)S(1)} copy-done((bf16[1280,160]{0,1:T(8,128)(2,1)S(1)}, bf16[1280,160]{0,1:T(8,128)(2,1)}, u32[]{:S(2)}) %copy-start.4) | copy-done | bytes 409624
  6.7 0.0 copy-start.5
  6.7 0.7 copy-done.5
  7.4 76.2 %shard_map.73 = bf16[384,1280]{1,0:T(8,128)(2,1)S(1)} custom-call(s32[1]{0:T(128)S(6)} %copy.9.die_ref, f32[1280]{0:T(1024)S(1)} %copy-done.5, bf16[384,1280]{1,0:T(8,128)(2,1)S(1)} %bitcast.4, bf16[2,384,1280]{2,1,0:T(8,128)(2,1)S(1)} %copy-done, bf16[160,1280]{1,0:T(8,128)(2,1)S(1)} %bitcast.5, bf16[160,2560]{1,0:T(8,128)(2,1)S(1)} %copy-done.2, ...), custom_call_target="tpu_custom_call" | custom-call | tf_op jit(solution)/shard_map/pallas_call | solution.py:210
  83.6 0.9 %copy.10 = bf16[1,384,1280]{2,1,0:T(8,128)(2,1)} copy(bf16[1,384,1280]{2,1,0:T(8,128)(2,1)S(1)} %bitcast.3) | data formatting | bytes 1966080
Async XLA Ops:
  0.7 1.5 %copy-start = (bf16[2,384,1280]{2,1,0:T(8,128)(2,1)S(1)}, bf16[2,384,1280]{2,1,0:T(8,128)(2,1)}, u32[]{:S(2)}) copy-start(bf16[2,384,1280]{2,1,0:T(8,128)(2,1)} %gold_hbm.1) | copy-start | bytes 5898244
  2.2 1.2 %copy-start.1 = (bf16[1,384,1280]{2,1,0:T(8,128)(2,1)S(1)}, bf16[1,384,1280]{2,1,0:T(8,128)(2,1)}, u32[]{:S(2)}) copy-start(bf16[1,384,1280]{2,1,0:T(8,128)(2,1)} %param.7) | copy-start | bytes 2949124
  3.4 1.1 %copy-start.2 = (bf16[160,2560]{1,0:T(8,128)(2,1)S(1)}, bf16[160,2560]{1,0:T(8,128)(2,1)}, u32[]{:S(2)}) copy-start(bf16[160,2560]{1,0:T(8,128)(2,1)} %p_hbm.1) | copy-start | bytes 2457604
  4.5 1.1 %copy-start.3 = (bf16[320,1280]{1,0:T(8,128)(2,1)S(1)}, bf16[320,1280]{1,0:T(8,128)(2,1)}, u32[]{:S(2)}) copy-start(bf16[320,1280]{1,0:T(8,128)(2,1)} %o_hbm.1) | copy-start | bytes 2457604
  5.7 1.0 %copy-start.4 = (bf16[1280,160]{0,1:T(8,128)(2,1)S(1)}, bf16[1280,160]{0,1:T(8,128)(2,1)}, u32[]{:S(2)}) copy-start(bf16[1280,160]{0,1:T(8,128)(2,1)} %param.13) | copy-start | bytes 1228804
  6.7 0.7 copy-start.5
